TPU v7x, 32 devices: a whole 2x2x4 slice. The times are simulated.
32 devices in a mesh: groups: 2 (over y), page: 4 (over z), tensor: 4 (over x, core).
Axes of the slice: x: 2, y: 2, z: 4, core: 2. Of those that a mesh axis runs over, the one named last changes fastest.
Arguments:
- query: bfloat16 [4096, 4096], P(('groups', 'page'), 'tensor'), parts along dimension 0, may hold values from -13 to 13
- memory: bfloat16 [2048, 1024], P(('groups', 'page'), 'tensor'), parts along dimension 0, may hold values from -20 to 20
- key_weight: bfloat16 [1024, 4096], P(None, 'tensor'), may hold values from -2.6 to 2.6
- value_weight: bfloat16 [1024, 4096], P(None, 'tensor'), may hold values from -0.1875 to 0.1875
- out_grad: bfloat16 [4096, 4096], P(('groups', 'page'), 'tensor'), parts along dimension 0, may hold values from -6 to 6
- mask_blocks: int32 [8, 3, 4, 2], P(('groups', 'page')), parts along dimension 0, may hold values from 0 to 1, as said below
Outputs:
- attended: bfloat16 [4096, 4096], P(('groups', 'page'), 'tensor'), parts along dimension 0
- query_grad: bfloat16 [4096, 4096], P(('groups', 'page'), 'tensor'), parts along dimension 0
- memory_grad: bfloat16 [2048, 1024], P(('groups', 'page'), 'tensor'), parts along dimension 0
There are 2 independent parts, one for each index of `groups`. A program takes and returns all parts, laid end to end along the dimension named above; an argument that names none is the same for every part. Nothing has to cross between parts.
Inputs may be any that keep to these rules, and one draw needn't show every extreme that they name: `mask_blocks`: for every page and every block of 128 query rows, at least one block of the page's own memory (slot 1) is marked.
All inputs are finite; a program needn't handle non-finite values.
Results may differ from a plain program's by a relative error of at most 0.02.
The roundings to bfloat16 on the way count: a program that leaves them out, or rounds other values in their place, can miss the bound.
Values may be sent and summed in bfloat16 or wider, within the bound.
A program may use at most 128 MiB of HBM per device.

v0:
```python
import math

import jax
import jax.numpy as jnp
from jax import lax
from jax.sharding import PartitionSpec as P

HD = 128


masked_score = -1e30


def padded(block, sides, width):
    for axis, dim in sides:
        count = lax.axis_size(axis)
        forward = [(i, i + 1) for i in range(count - 1)]
        backward = [(target, source) for source, target in forward]
        low = lax.ppermute(
            lax.slice_in_dim(block, block.shape[dim] - width, None, axis=dim), axis, forward
        )
        high = lax.ppermute(lax.slice_in_dim(block, 0, width, axis=dim), axis, backward)
        block = jnp.concatenate([low, block, high], axis=dim)
    return block


def from_behind(x, axis, by):
    devices = lax.axis_size(axis)
    pairs = [(i, i + by) for i in range(devices) if 0 <= i + by < devices]
    return lax.ppermute(x, axis, pairs)


def back_project(key_part, value_part, key_weight, value_weight):
    dims = (((1,), (1,)), ((), ()))
    return lax.dot_general(
        key_part, key_weight, dims, preferred_element_type=jnp.float32
    ) + lax.dot_general(value_part, value_weight, dims, preferred_element_type=jnp.float32)


def on_device(query, memory, key_weight, value_weight, out_grad, mask_blocks):
    token_rows = query.shape[0]
    features = query.shape[1]
    head_count = features // HD
    memory_rows = memory.shape[0]
    page_index = lax.axis_index("page")
    page_total = lax.axis_size("page")
    memory_rim = padded(memory, (("page", 0),), memory_rows)
    wide_memory = lax.all_gather(memory_rim, "tensor", axis=1, tiled=True)
    key_slab = jnp.dot(wide_memory, key_weight, preferred_element_type=jnp.float32).astype(
        jnp.bfloat16
    )
    value_slab = jnp.dot(wide_memory, value_weight, preferred_element_type=jnp.float32).astype(
        jnp.bfloat16
    )
    sources = page_index + jnp.arange(3, dtype=jnp.int32) - 1
    source_live = ((sources >= 0) & (sources < page_total)).astype(jnp.float32)
    block_grid = mask_blocks[0].astype(jnp.float32) * source_live[:, None, None]
    query_blocks = block_grid.shape[1]
    memory_blocks = block_grid.shape[2]
    block_size = token_rows // query_blocks
    spread_grid = jnp.transpose(block_grid, (1, 0, 2))[:, None, :, :, None]
    visible = jnp.broadcast_to(
        spread_grid, (query_blocks, block_size, 3, memory_blocks, block_size)
    ).reshape(token_rows, 3 * memory_rows)
    score_scale = 1.0 / math.sqrt(HD)
    query_heads = query.reshape(token_rows, head_count, HD)
    key_heads = key_slab.reshape(3 * memory_rows, head_count, HD)
    value_heads = value_slab.reshape(3 * memory_rows, head_count, HD)
    scores = (
        jnp.einsum("thd,khd->htk", query_heads, key_heads, preferred_element_type=jnp.float32)
        * score_scale
    )
    scores = jnp.where(visible[None] > 0, scores, masked_score)
    row_max = jnp.max(scores, axis=2, keepdims=True)
    exponent = jnp.exp(scores - row_max)
    weights = exponent / jnp.sum(exponent, axis=2, keepdims=True)
    rounded_weights = weights.astype(jnp.bfloat16)
    mixed = jnp.einsum(
        "htk,khd->thd", rounded_weights, value_heads, preferred_element_type=jnp.float32
    )
    attended = mixed.reshape(token_rows, features).astype(jnp.bfloat16)
    grad_rows = out_grad.reshape(token_rows, head_count, HD)
    weight_grad = jnp.einsum(
        "thd,khd->htk", grad_rows, value_heads, preferred_element_type=jnp.float32
    )
    row_inner = jnp.sum(weights * weight_grad, axis=2, keepdims=True)
    score_grad = (weights * (weight_grad - row_inner) * score_scale).astype(jnp.bfloat16)
    query_grad = jnp.einsum(
        "htk,khd->thd", score_grad, key_heads, preferred_element_type=jnp.float32
    )
    query_grad = query_grad.reshape(token_rows, features).astype(jnp.bfloat16)
    key_piece = jnp.einsum(
        "htk,thd->khd", score_grad, query_heads, preferred_element_type=jnp.float32
    )
    key_piece = key_piece.reshape(3 * memory_rows, features).astype(jnp.bfloat16)
    value_piece = jnp.einsum(
        "htk,thd->khd", rounded_weights, grad_rows, preferred_element_type=jnp.float32
    )
    value_piece = value_piece.reshape(3 * memory_rows, features).astype(jnp.bfloat16)
    toward_previous = jnp.stack([key_piece[:memory_rows], value_piece[:memory_rows]])
    toward_next = jnp.stack([key_piece[2 * memory_rows :], value_piece[2 * memory_rows :]])
    from_next = from_behind(toward_previous, "page", -1)
    from_prev = from_behind(toward_next, "page", 1)
    partial_value = back_project(
        key_piece[memory_rows : 2 * memory_rows],
        value_piece[memory_rows : 2 * memory_rows],
        key_weight,
        value_weight,
    )
    partial_value = partial_value + back_project(
        from_next[0], from_next[1], key_weight, value_weight
    )
    partial_value = partial_value + back_project(
        from_prev[0], from_prev[1], key_weight, value_weight
    )
    summed = lax.psum_scatter(
        partial_value.astype(jnp.bfloat16), "tensor", scatter_dimension=1, tiled=True
    )
    return (attended, query_grad, summed)


def solution(mesh):
    placed = (
        P(("groups", "page"), "tensor"),
        P(("groups", "page"), "tensor"),
        P(None, "tensor"),
        P(None, "tensor"),
        P(("groups", "page"), "tensor"),
        P(("groups", "page"), None, None, None),
    )
    return jax.shard_map(
        on_device,
        mesh=mesh,
        in_specs=placed,
        out_specs=(
            P(("groups", "page"), "tensor"),
            P(("groups", "page"), "tensor"),
            P(("groups", "page"), "tensor"),
        ),
        check_vma=False,
    )
```

profile of v0, /device:TPU:0, one launch (start us, length us, event | category | flops | bytes accessed | tf_op | source)
XLA Modules:
  0.0 164.3 jit_solution(5907997166472424290)
XLA Ops:
  7.2 1.4 collective-permute-start.1
  8.7 5.6 %collective-permute-start = (bf16[256,256]{1,0:T(8,128)(2,1)}, bf16[256,256]{1,0:T(8,128)(2,1)S(1)}, u32[]{:S(2)}, u32[]{:S(2)}) collective-permute-start(bf16[256,256]{1,0:T(8,128)(2,1)} %param.7), channel_id=1, source_target_pairs={{0,4},{4,8},{8,12},{1,5},{5,9},{9,13},{2,6},{6,10},{10,14},{3,7},{... | collective-permute-start | bytes 393224 | tf_op jit(solution)/shard_map/ppermute | solution.py:19
  14.2 1.8 %collective-permute-done.1 = bf16[256,256]{1,0:T(8,128)(2,1)S(1)} collective-permute-done((bf16[256,256]{1,0:T(8,128)(2,1)}, bf16[256,256]{1,0:T(8,128)(2,1)S(1)}, u32[]{:S(2)}, u32[]{:S(2)}) %collective-permute-start.1) | collective-permute-done | bytes 131104 | tf_op jit(solution)/shard_map/ppermute | solution.py:22
  16.0 1.3 collective-permute-done
  17.3 1.7 %pad_maximum_fusion.2 = bf16[768,256]{1,0:T(8,128)(2,1)} fusion(bf16[256,256]{1,0:T(8,128)(2,1)S(1)} %collective-permute-done.1, bf16[256,256]{1,0:T(8,128)(2,1)} %param.7, bf16[256,256]{1,0:T(8,128)(2,1)S(1)} %collective-permute-done), kind=kLoop, calls=%fused_computation.51 | loop fusion | flops 1179648 | bytes 786432 | tf_op jit(solution)/shard_map/concatenate | solution.py:23
  19.0 0.8 compare_bitcast_fusion
  20.3 2.3 %copy.28 = bf16[512,1024]{0,1:T(8,128)(2,1)} copy(bf16[512,1024]{1,0:T(8,128)(2,1)} %param.6) | data formatting | bytes 2097152 | tf_op jit(solution)/shard_map/reshape | solution.py:66
  22.6 1.5 copy.29
  24.1 17.2 %all-gather.2.cloned.1.call-done = bf16[768,1024]{1,0:T(8,128)(2,1)} async-done(((bf16[768,256]{1,0:T(8,128)(2,1)}), bf16[768,1024]{1,0:T(8,128)(2,1)}) %all-gather.2.cloned.1.call-update) | async-done | bytes 1572880 | tf_op jit(solution)/shard_map/all_gather | solution.py:48
  41.2 5.0 %convolution_convert_fusion = bf16[768,1024]{1,0:T(8,128)(2,1)} fusion(bf16[768,1024]{1,0:T(8,128)(2,1)} %all-gather.2.cloned.1.call-done, bf16[1024,1024]{1,0:T(8,128)(2,1)} %param.8), kind=kOutput, calls=%fused_computation.23 | convolution fusion | flops 1611399168 | bytes 5242880 | tf_op jit(solution)/shard_map/dot_general | solution.py:49
  46.3 2.6 %copy.27 = bf16[768,1024]{0,1:T(8,128)(2,1)} copy(bf16[768,1024]{1,0:T(8,128)(2,1)} %convolution_convert_fusion) | data formatting | bytes 3145728 | tf_op jit(solution)/shard_map/reshape | solution.py:67
  48.9 3.2 %fusion.26 = bf16[96,8,8,128]{3,2,1,0:T(8,128)(2,1)S(1)} fusion(bf16[768,1024]{1,0:T(8,128)(2,1)} %all-gather.2.cloned.1.call-done, bf16[1024,1024]{1,0:T(8,128)(2,1)S(1)} %copy-done), kind=kOutput, calls=%fused_computation.30 | convolution fusion | flops 1611399168 | bytes 5242880 | tf_op jit(solution)/shard_map/dot_general | solution.py:52
  52.1 6.3 %fusion.21 = f32[8,768,512]{2,1,0:T(8,128)} fusion(bf16[512,8,128]{0,2,1:T(8,128)(2,1)S(1)} %bitcast.118, bf16[96,8,8,128]{3,2,1,0:T(8,128)(2,1)S(1)} %fusion.26), kind=kOutput, calls=%fused_computation.26 | convolution fusion | flops 805306368 | bytes 15204352 | tf_op jit(solution)/shard_map/thd,khd->htk/dot_general | solution.py:83
  58.4 11.0 %fusion.51 = (f32[8,512]{1,0:T(8,128)S(1)}, f32[8,512,768]{1,2,0:T(8,128)}) fusion(pred[512,768]{0,1:T(8,128)(4,1)S(1)} %bitcast.133, bf16[768,8,128]{0,2,1:T(8,128)(2,1)} %bitcast.126, bf16[512,8,128]{0,2,1:T(8,128)(2,1)} %bitcast.129), kind=kOutput, calls=%fused_computation.63 | convolution fusion | flops 817890048 | bytes 15613952 | tf_op jit(solution)/shard_map/sub | solution.py:75
  69.4 8.0 %fusion.23 = bf16[768,8,128]{0,2,1:T(8,128)(2,1)} fusion(bf16[512,8,128]{0,2,1:T(8,128)(2,1)S(1)} %bitcast.119, f32[8,512,768]{1,2,0:T(8,128)} %get-tuple-element.13, f32[8,512]{1,0:T(8,128)S(1)} %get-tuple-element.12), kind=kOutput, calls=%fused_computation.29 | convolution fusion | flops 812384256 | bytes 15220736 | tf_op jit(solution)/shard_map/htk,thd->khd/dot_general | solution.py:96
  77.4 18.9 %fusion.27 = bf16[768,8,128]{0,2,1:T(8,128)(2,1)} fusion(bf16[512,8,128]{0,2,1:T(8,128)(2,1)} %bitcast.130, f32[8,768,512]{2,1,0:T(8,128)} %fusion.21, f32[8,512,768]{1,2,0:T(8,128)} %get-tuple-element.13, f32[8,512]{1,0:T(8,128)S(1)} %get-tuple-element.12), kind=kOutput, calls=%fused_computation.31 | convolution fusion | flops 828117760 | bytes 27803648 | tf_op jit(solution)/shard_map/htk,thd->khd/dot_general | solution.py:92
  96.3 1.6 fusion.49
  97.9 0.3 copy-done.3
  98.5 1.4 collective-permute-start.2
  100.0 4.6 %collective-permute-start.3 = (bf16[2,256,1024]{1,2,0:T(8,128)(2,1)S(1)}, bf16[2,256,1024]{1,2,0:T(8,128)(2,1)S(1)}, u32[]{:S(2)}, u32[]{:S(2)}) collective-permute-start(bf16[2,256,1024]{1,2,0:T(8,128)(2,1)S(1)} %pad_maximum_fusion.1), channel_id=1, source_target_pairs={{0,4},{4,8},{8,12},{1,5},{5,9},{9,13},{2,6},{6,10},{10,14},{3,7},{... | collective-permute-start | bytes 3145736 | tf_op jit(solution)/shard_map/ppermute | solution.py:30
  104.6 0.8 fusion.52
  105.4 0.8 convolution_add_fusion.2
  106.2 19.6 %collective-permute-done.2 = bf16[2,256,1024]{1,2,0:T(8,128)(2,1)S(1)} collective-permute-done((bf16[2,256,1024]{1,2,0:T(8,128)(2,1)S(1)}, bf16[2,256,1024]{1,2,0:T(8,128)(2,1)S(1)}, u32[]{:S(2)}, u32[]{:S(2)}) %collective-permute-start.2) | collective-permute-done | bytes 1048608 | tf_op jit(solution)/shard_map/ppermute | solution.py:30
  125.8 0.8 fusion.42
  126.6 0.5 collective-permute-done.3
  127.1 0.8 fusion.41
  127.9 0.8 fusion.37
  128.7 1.6 fusion.38
  130.3 6.3 %fusion.28 = bf16[8,128,512]{2,1,0:T(8,128)(2,1)S(1)} fusion(bf16[96,8,8,128]{3,2,1,0:T(8,128)(2,1)} %copy-done.2, f32[8,512,768]{1,2,0:T(8,128)} %get-tuple-element.13, f32[8,512]{1,0:T(8,128)S(1)} %get-tuple-element.12), kind=kOutput, calls=%fused_computation.32 | convolution fusion | flops 812122112 | bytes 15220736 | tf_op jit(solution)/shard_map/htk,khd->thd/dot_general | solution.py:78
  136.6 1.3 copy.21
  137.9 18.3 %fusion.33 = bf16[8,128,512]{2,1,0:T(8,128)(2,1)S(1)} fusion(bf16[768,8,128]{0,2,1:T(8,128)(2,1)} %bitcast.127, f32[8,768,512]{2,1,0:T(8,128)} %fusion.21, f32[8,512,768]{1,2,0:T(8,128)} %get-tuple-element.13, f32[8,512]{1,0:T(8,128)S(1)} %get-tuple-element.12), kind=kOutput, calls=%fused_computation.33 | convolution fusion | flops 827855616 | bytes 27803648 | tf_op jit(solution)/shard_map/htk,khd->thd/dot_general | solution.py:88
  156.1 1.3 copy.22
  (18 shorter events, 1.0 us)
Async XLA Ops:
  7.2 41.8 %copy-start = (bf16[1024,1024]{1,0:T(8,128)(2,1)S(1)}, bf16[1024,1024]{1,0:T(8,128)(2,1)}, u32[]{:S(2)}) copy-start(bf16[1024,1024]{1,0:T(8,128)(2,1)} %param.9) | copy-start | bytes 6291460
  7.2 34.1 %all-gather.2.cloned.1.call-start = ((), (), s32[]{:S(2)}) async-start(), calls=%async_computation.1 | async-start | bytes 1966080 | tf_op jit(solution)/shard_map/all_gather | solution.py:48
  7.2 8.8 %collective-permute-start.1 = (bf16[256,256]{1,0:T(8,128)(2,1)}, bf16[256,256]{1,0:T(8,128)(2,1)S(1)}, u32[]{:S(2)}, u32[]{:S(2)}) collective-permute-start(bf16[256,256]{1,0:T(8,128)(2,1)} %param.7), channel_id=1, source_target_pairs={{4,0},{8,4},{12,8},{5,1},{9,5},{13,9},{6,2},{10,6},{14,10},{7,3},{... | collective-permute-start | bytes 393224 | tf_op jit(solution)/shard_map/ppermute | solution.py:22
  8.7 8.6 %collective-permute-start = (bf16[256,256]{1,0:T(8,128)(2,1)}, bf16[256,256]{1,0:T(8,128)(2,1)S(1)}, u32[]{:S(2)}, u32[]{:S(2)}) collective-permute-start(bf16[256,256]{1,0:T(8,128)(2,1)} %param.7), channel_id=1, source_target_pairs={{0,4},{4,8},{8,12},{1,5},{5,9},{9,13},{2,6},{6,10},{10,14},{3,7},{... | collective-permute-start | bytes 393224 | tf_op jit(solution)/shard_map/ppermute | solution.py:19
  19.0 138.5 %reduce-scatter.2.cloned.1.call-start = ((), (), s32[]{:S(2)}) async-start(), calls=%async_computation.2 | async-start | bytes 655360 | tf_op jit(solution)/shard_map/reduce_scatter | solution.py:116
  52.1 6.3 %copy-start.2 = (bf16[96,8,8,128]{3,2,1,0:T(8,128)(2,1)}, bf16[96,8,8,128]{3,2,1,0:T(8,128)(2,1)S(1)}, u32[]{:S(2)}) copy-start(bf16[96,8,8,128]{3,2,1,0:T(8,128)(2,1)S(1)} %fusion.26) | copy-start | bytes 4718596
  96.3 1.9 %copy-start.3 = (bf16[768,8,128]{0,2,1:T(8,128)(2,1)S(1)}, bf16[768,8,128]{0,2,1:T(8,128)(2,1)}, u32[]{:S(2)}) copy-start(bf16[768,8,128]{0,2,1:T(8,128)(2,1)} %fusion.23) | copy-start | bytes 4718596
  98.2 6.4 %copy-start.1 = (bf16[1024,1024]{1,0:T(8,128)(2,1)S(1)}, bf16[1024,1024]{1,0:T(8,128)(2,1)}, u32[]{:S(2)}) copy-start(bf16[1024,1024]{1,0:T(8,128)(2,1)} %param.8) | copy-start | bytes 6291460
  98.5 27.3 %collective-permute-start.2 = (bf16[2,256,1024]{1,2,0:T(8,128)(2,1)S(1)}, bf16[2,256,1024]{1,2,0:T(8,128)(2,1)S(1)}, u32[]{:S(2)}, u32[]{:S(2)}) collective-permute-start(bf16[2,256,1024]{1,2,0:T(8,128)(2,1)S(1)} %pad_maximum_fusion), channel_id=1, source_target_pairs={{4,0},{8,4},{12,8},{5,1},{9,5},{13,9},{6,2},{10,6},{14,10},{7,3},{... | collective-permute-start | bytes 3145736 | tf_op jit(solution)/shard_map/ppermute | solution.py:30
  100.0 27.1 %collective-permute-start.3 = (bf16[2,256,1024]{1,2,0:T(8,128)(2,1)S(1)}, bf16[2,256,1024]{1,2,0:T(8,128)(2,1)S(1)}, u32[]{:S(2)}, u32[]{:S(2)}) collective-permute-start(bf16[2,256,1024]{1,2,0:T(8,128)(2,1)S(1)} %pad_maximum_fusion.1), channel_id=1, source_target_pairs={{0,4},{4,8},{8,12},{1,5},{5,9},{9,13},{2,6},{6,10},{10,14},{3,7},{... | collective-permute-start | bytes 3145736 | tf_op jit(solution)/shard_map/ppermute | solution.py:30
Sparse Core Ops, SparseCore 0:
  19.1 22.1 all-gather.1
  130.4 22.8 reduce-scatter.1
where the time goes:
time: 165 us; the launch traced here: 164 us
  matrix products  82.4 us (50%)
  waiting for transfers between devices  40.4 us (24%)
  between operations  14.2 us (9%)
  starting transfers between devices  13.1 us (8%)
  local copies, waits for them, and re-layouts  11.6 us (7%)
  other arithmetic  2.64 us (2%)
    ppermute x2, waiting for transfers between devices, from_behind(): return lax.ppermute(x, axis, pairs)  20.1 us
    dot_general x1, matrix products, on_device(): jnp.einsum('htk,thd->khd', score_grad, query_heads, preferred_element_typ...  18.9 us
    dot_general x1, matrix products, on_device(): jnp.einsum('htk,khd->thd', score_grad, key_heads, preferred_element_type=...  18.3 us
    all_gather x1, waiting for transfers between devices, on_device(): wide_memory = lax.all_gather(memory_rim, 'tensor', axis=1, tiled=True)  17.2 us
    sub x1, matrix products, on_device(): exponent = jnp.exp(scores - row_max)  11 us
    dot_general x1, matrix products, on_device(): jnp.einsum('htk,thd->khd', rounded_weights, grad_rows, preferred_element_...  7.97 us
    dot_general x1, matrix products, on_device(): jnp.einsum('htk,khd->thd', rounded_weights, value_heads, preferred_elemen...  6.29 us
    dot_general x1, matrix products, on_device(): jnp.einsum('thd,khd->htk', grad_rows, value_heads, preferred_element_type...  6.26 us
  transfers between devices with their start and end apart: 6, of which 5 were waited for; matrix products, arithmetic and copies ran while one was open for 21% of the time, Pallas kernels for 0%

commit v1 on v0

v1 whole, which is shorter than its diff:
```python
import functools
import math

import jax
import jax.numpy as jnp
from jax import lax
from jax.experimental import pallas as pl
from jax.experimental.pallas import tpu as pltpu
from jax.sharding import PartitionSpec as P

HD = 128
MESH = pl.DeviceIdType.MESH
VMEM_LIMIT = 56 * 1024 * 1024
F32 = jnp.float32
BF16 = jnp.bfloat16


def place():
    page = lax.axis_index("page")
    tensor = lax.axis_index("tensor")
    core = lax.rem(tensor, 2)
    return page, tensor, core, tensor + 1 - 2 * core


def greet(pages, tensors):
    page, tensor, core, sibling = place()
    barrier = pltpu.get_barrier_semaphore()
    chips = tensors // 2

    def signal(where):
        pl.semaphore_signal(barrier, inc=1, device_id=where, device_id_type=MESH)

    signal({"tensor": sibling})
    for d in range(1, chips):
        signal({"tensor": lax.rem(tensor + 2 * d, tensors)})

    @pl.when(page > 0)
    def _():
        signal({"page": page - 1})

    @pl.when(page < pages - 1)
    def _():
        signal({"page": page + 1})

    def wait():
        at_end = jnp.where(page > 0, 1, 0) + jnp.where(page < pages - 1, 1, 0)
        pl.semaphore_wait(barrier, chips + at_end)

    return wait


def remote(src, dst, send, recv, where):
    return pltpu.make_async_remote_copy(
        src_ref=src, dst_ref=dst, send_sem=send, recv_sem=recv, device_id=where, device_id_type=MESH
    )


def project_kernel(
    pages, tensors, mem_ref, wk_hbm, wv_hbm, k_hbm, v_hbm,
    gathered, wk, wv, keys, values, load_sem, store_sem, send_sem, recv_sem,
):
    page, tensor, core, sibling = place()
    chips = tensors // 2
    rows, width = mem_ref.shape
    features = wk.shape[1]
    tile = min(256, features)

    loads = [
        pltpu.make_async_copy(wk_hbm, wk, load_sem.at[0]),
        pltpu.make_async_copy(wv_hbm, wv, load_sem.at[1]),
    ]
    wait_barrier = greet(pages, tensors)
    for load in loads:
        load.start()
    gathered[1, tensor] = mem_ref[...]
    has_prev = page > 0
    has_next = page < pages - 1

    def to_sibling(src, slot, owner):
        return remote(src, gathered.at[slot, owner], send_sem.at[slot, owner], recv_sem.at[slot, owner], {"tensor": sibling})

    def to_chip(src, d):
        there = lax.rem(tensor + 2 * d, tensors)
        return remote(src, gathered.at[1, tensor], send_sem.at[3, there], recv_sem.at[1, tensor], {"tensor": there})

    def to_next(src, owner):
        return remote(src, gathered.at[0, owner], send_sem.at[4, owner], recv_sem.at[0, owner], {"page": page + 1})

    def to_prev(src, owner):
        return remote(src, gathered.at[2, owner], send_sem.at[5, owner], recv_sem.at[2, owner], {"page": page - 1})

    def arrived(slot, owner):
        remote(
            gathered.at[slot, owner], gathered.at[slot, owner], send_sem.at[0, owner],
            recv_sem.at[slot, owner], {"tensor": sibling},
        ).wait_recv()

    def spread(src, owner):
        @pl.when(has_next)
        def _():
            to_next(src, owner).start()

        @pl.when(has_prev)
        def _():
            to_prev(src, owner).start()

    wait_barrier()
    for d in range(1, chips):
        to_chip(mem_ref, d).start()
    spread(mem_ref, tensor)
    to_sibling(mem_ref, 1, tensor).start()
    peers = [lax.rem(tensor + 2 * d, tensors) for d in range(chips)]
    for owner in peers[1:]:
        arrived(1, owner)
        spread(gathered.at[1, owner], owner)
        to_sibling(gathered.at[1, owner], 1, owner).start()

    stores = {}

    def project(slot):
        def step(i, _):
            columns = pl.ds(pl.multiple_of(i * tile, tile), tile)
            whole = jnp.concatenate([gathered[slot, owner] for owner in range(tensors)], axis=1)
            keys[slot, :, columns] = jnp.dot(whole, wk[:, columns], preferred_element_type=F32).astype(BF16)
            values[slot, :, columns] = jnp.dot(whole, wv[:, columns], preferred_element_type=F32).astype(BF16)
            return 0

        lax.fori_loop(0, features // tile, step, 0)

    def write(slot):
        span = pl.ds(slot * rows, rows)
        stores[slot] = [
            pltpu.make_async_copy(keys.at[slot], k_hbm.at[span], store_sem.at[slot, 0]),
            pltpu.make_async_copy(values.at[slot], v_hbm.at[span], store_sem.at[slot, 1]),
        ]
        for store in stores[slot]:
            store.start()

    def other(owner):
        return owner + 1 - 2 * lax.rem(owner, 2)

    def pass_on(k):
        @pl.when(has_prev)
        def _():
            arrived(0, peers[k])
            to_sibling(gathered.at[0, peers[k]], 0, peers[k]).start()

        @pl.when(has_next)
        def _():
            arrived(2, peers[k])
            to_sibling(gathered.at[2, peers[k]], 2, peers[k]).start()

    for owner in peers:
        arrived(1, other(owner))
    for load in loads:
        load.wait()
    project(1)
    write(1)
    for k in range(chips):
        pass_on(k)
    for slot, there in ((0, has_prev), (2, has_next)):
        @pl.when(there)
        def _():
            for owner in peers:
                arrived(slot, other(owner))
            project(slot)

        @pl.when(jnp.logical_not(there))
        def _():
            keys[slot] = jnp.zeros(keys.shape[1:], BF16)
            values[slot] = jnp.zeros(values.shape[1:], BF16)

        write(slot)

    for d in range(1, chips):
        to_chip(mem_ref, d).wait_send()
    for owner in peers:
        to_sibling(mem_ref, 1, owner).wait_send()

        @pl.when(has_next)
        def _():
            to_next(mem_ref, owner).wait_send()
            to_sibling(mem_ref, 2, owner).wait_send()

        @pl.when(has_prev)
        def _():
            to_prev(mem_ref, owner).wait_send()
            to_sibling(mem_ref, 0, owner).wait_send()
    for slot in (1, 0, 2):
        for store in stores[slot]:
            store.wait()


def attend_kernel(pages, mask_ref, q_ref, g_ref, k_ref, v_ref, att_ref, qg_ref, kp_ref, vp_ref):
    page = lax.axis_index("page")
    slots, query_blocks, memory_blocks = mask_ref.shape[1:]
    block = q_ref.shape[0] // query_blocks
    scale = 1.0 / math.sqrt(HD)
    rate = scale * math.log2(math.e)
    nt = (((1,), (1,)), ((), ()))
    tn = (((0,), (0,)), ((), ()))
    for head in range(q_ref.shape[1] // HD):
        cols = slice(head * HD, (head + 1) * HD)
        q, g, k, v = q_ref[:, cols], g_ref[:, cols], k_ref[:, cols], v_ref[:, cols]
        scores = lax.dot_general(k, q, nt, preferred_element_type=F32)
        weight_grad = lax.dot_general(v, g, nt, preferred_element_type=F32)
        rounded, score_grads = [], []
        for tb in range(query_blocks):
            span = slice(tb * block, (tb + 1) * block)
            parts = []
            for slot in range(slots):
                source = page + (slot - 1)
                live = jnp.logical_and(source >= 0, source < pages)
                for mb in range(memory_blocks):
                    seen = jnp.logical_and(mask_ref[0, slot, tb, mb] > 0, live)
                    low = (slot * memory_blocks + mb) * block
                    parts.append(scores[low : low + block, span] + jnp.where(seen, 0.0, -1e30).astype(F32))
            biased = jnp.concatenate(parts, axis=0)
            top = jnp.max(biased, axis=0, keepdims=True)
            exponent = jnp.exp2((biased - top) * rate)
            weights = exponent * (1.0 / jnp.sum(exponent, axis=0, keepdims=True))
            rounded.append(weights.astype(BF16))
            grad = weight_grad[:, span]
            inner = jnp.sum(weights * grad, axis=0, keepdims=True)
            score_grads.append((weights * (grad - inner)).astype(BF16))
        rounded = jnp.concatenate(rounded, axis=1)
        score_grad = jnp.concatenate(score_grads, axis=1)
        att = lax.dot_general(v, rounded, tn, preferred_element_type=F32)
        att_ref[:, cols] = att.T.astype(BF16)
        vp_ref[:, cols] = jnp.dot(rounded, g, preferred_element_type=F32).astype(BF16)
        qg = lax.dot_general(k, score_grad, tn, preferred_element_type=F32) * scale
        qg_ref[:, cols] = qg.T.astype(BF16)
        kp_ref[:, cols] = (jnp.dot(score_grad, q, preferred_element_type=F32) * scale).astype(BF16)


def reduce_kernel(
    pages, tensors, kp_hbm, vp_hbm, wk_hbm, wv_hbm, out_ref,
    kp, vp, wk, wv, own, stage, from_core, page_stage, from_page, chip_stage, from_chip,
    load_sem, core_send, core_recv, page_send, page_recv, chip_send, chip_recv,
):
    page, tensor, core, sibling = place()
    chips = tensors // 2
    chip = tensor // 2
    rows, width = out_ref.shape
    nt = (((1,), (1,)), ((), ()))
    wait_barrier = greet(pages, tensors)
    loads = [
        pltpu.make_async_copy(wk_hbm, wk, load_sem.at[0]),
        pltpu.make_async_copy(kp_hbm, kp, load_sem.at[1]),
        pltpu.make_async_copy(wv_hbm, wv, load_sem.at[2]),
        pltpu.make_async_copy(vp_hbm, vp, load_sem.at[3]),
    ]
    for load in loads:
        load.start()

    def partial(slot, group):
        take = pl.ds(pl.multiple_of(group * width, width), width)
        span = slice(slot * rows, (slot + 1) * rows)
        return lax.dot_general(kp[span], wk[take], nt, preferred_element_type=F32) + lax.dot_general(
            vp[span], wv[take], nt, preferred_element_type=F32
        )

    def to_core(slot, there):
        return remote(
            stage.at[slot, there], from_core.at[slot, there], core_send.at[slot, there],
            core_recv.at[slot, there], {"tensor": sibling},
        )

    def to_page(side, there):
        return remote(
            page_stage.at[side, there], from_page.at[side, there], page_send.at[side, there],
            page_recv.at[side, there], {"page": page - 1 + 2 * side},
        )

    def to_chip(there):
        return remote(
            chip_stage.at[there], from_chip.at[chip], chip_send.at[there], chip_recv.at[chip],
            {"tensor": 2 * there + core},
        )

    def chip_arrived(there):
        remote(
            chip_stage.at[there], from_chip.at[there], chip_send.at[there], chip_recv.at[there],
            {"tensor": 2 * there + core},
        ).wait_recv()

    order = [lax.rem(chip + 1 + k, chips) for k in range(chips)]

    def partials(slot, before_send=None):
        for there in order:
            stage[slot, there] = partial(slot, 2 * there + 1 - core).astype(BF16)
            if before_send is not None:
                before_send()
                before_send = None
            to_core(slot, there).start()
        for there in order:
            own[slot, there] = partial(slot, 2 * there + core)

    for load in loads:
        load.wait()
    sides = (page > 0, page < pages - 1)
    for side in (0, 1):
        slot = 2 * side
        partials(slot, wait_barrier if side == 0 else None)
        for there in order:
            to_core(slot, there).wait_recv()

            @pl.when(sides[side])
            def _():
                page_stage[side, there] = (own[slot, there] + from_core[slot, there].astype(F32)).astype(BF16)
                to_page(side, there).start()
    partials(1)
    for there in order:
        to_core(1, there).wait_recv()
        own[1, there] += from_core[1, there].astype(F32)
    for there in order:
        for side in (0, 1):
            @pl.when(sides[1 - side])
            def _():
                to_page(side, there).wait_recv()
                own[1, there] += from_page[side, there].astype(F32)

        if there is not order[-1]:
            chip_stage[there] = own[1, there].astype(BF16)
            to_chip(there).start()
    total = own[1, chip]
    for there in order[:-1]:
        chip_arrived(there)
        total = total + from_chip[there].astype(F32)
    out_ref[...] = total.astype(BF16)
    for there in order:
        for slot in range(3):
            to_core(slot, there).wait_send()
        for side in (0, 1):
            @pl.when(sides[side])
            def _():
                to_page(side, there).wait_send()

        if there is not order[-1]:
            to_chip(there).wait_send()


def on_device(pages, tensors, query, memory, key_weight, value_weight, out_grad, mask_blocks):
    tokens, features = query.shape
    rows, width = memory.shape
    depth = key_weight.shape[0]
    chips = tensors // 2
    anywhere = pl.BlockSpec(memory_space=pl.ANY)
    in_vmem = pl.BlockSpec(memory_space=pltpu.VMEM)
    dma = pltpu.SemaphoreType.DMA
    keys, values = pl.pallas_call(
        functools.partial(project_kernel, pages, tensors),
        out_shape=[jax.ShapeDtypeStruct((3 * rows, features), BF16)] * 2,
        in_specs=[in_vmem, anywhere, anywhere],
        out_specs=[anywhere, anywhere],
        scratch_shapes=[
            pltpu.VMEM((3, tensors, rows, width), BF16),
            pltpu.VMEM((depth, features), BF16),
            pltpu.VMEM((depth, features), BF16),
            pltpu.VMEM((3, rows, features), BF16),
            pltpu.VMEM((3, rows, features), BF16),
            dma((2,)),
            dma((3, 2)),
            dma((6, tensors)),
            dma((3, tensors)),
        ],
        compiler_params=pltpu.CompilerParams(
            collective_id=0, has_side_effects=True, vmem_limit_bytes=VMEM_LIMIT
        ),
        name="gather_project",
    )(memory, key_weight, value_weight)

    heads = 1
    step = heads * HD
    column = lambda i: (0, i)
    attended, query_grad, key_piece, value_piece = pl.pallas_call(
        functools.partial(attend_kernel, pages),
        grid=(features // step,),
        out_shape=[jax.ShapeDtypeStruct((tokens, features), BF16)] * 2
        + [jax.ShapeDtypeStruct((3 * rows, features), BF16)] * 2,
        in_specs=[
            pl.BlockSpec(memory_space=pltpu.SMEM),
            pl.BlockSpec((tokens, step), column),
            pl.BlockSpec((tokens, step), column),
            pl.BlockSpec((3 * rows, step), column),
            pl.BlockSpec((3 * rows, step), column),
        ],
        out_specs=[
            pl.BlockSpec((tokens, step), column),
            pl.BlockSpec((tokens, step), column),
            pl.BlockSpec((3 * rows, step), column),
            pl.BlockSpec((3 * rows, step), column),
        ],
        compiler_params=pltpu.CompilerParams(vmem_limit_bytes=VMEM_LIMIT),
        name="attend",
    )(mask_blocks, query, out_grad, keys, values)

    memory_grad = pl.pallas_call(
        functools.partial(reduce_kernel, pages, tensors),
        out_shape=jax.ShapeDtypeStruct((rows, width), BF16),
        in_specs=[anywhere] * 4,
        out_specs=in_vmem,
        scratch_shapes=[
            pltpu.VMEM((3 * rows, features), BF16),
            pltpu.VMEM((3 * rows, features), BF16),
            pltpu.VMEM((depth, features), BF16),
            pltpu.VMEM((depth, features), BF16),
            pltpu.VMEM((3, chips, rows, width), F32),
            pltpu.VMEM((3, chips, rows, width), BF16),
            pltpu.VMEM((3, chips, rows, width), BF16),
            pltpu.VMEM((2, chips, rows, width), BF16),
            pltpu.VMEM((2, chips, rows, width), BF16),
            pltpu.VMEM((chips, rows, width), BF16),
            pltpu.VMEM((chips, rows, width), BF16),
            dma((4,)),
            dma((3, chips)),
            dma((3, chips)),
            dma((2, chips)),
            dma((2, chips)),
            dma((chips,)),
            dma((chips,)),
        ],
        compiler_params=pltpu.CompilerParams(
            collective_id=1, has_side_effects=True, vmem_limit_bytes=VMEM_LIMIT
        ),
        name="back_project_reduce",
    )(key_piece, value_piece, key_weight, value_weight)
    return attended, query_grad, memory_grad


def solution(mesh):
    placed = (
        P(("groups", "page"), "tensor"),
        P(("groups", "page"), "tensor"),
        P(None, "tensor"),
        P(None, "tensor"),
        P(("groups", "page"), "tensor"),
        P(("groups", "page"), None, None, None),
    )
    return jax.shard_map(
        functools.partial(on_device, mesh.shape["page"], mesh.shape["tensor"]),
        mesh=mesh,
        in_specs=placed,
        out_specs=(
            P(("groups", "page"), "tensor"),
            P(("groups", "page"), "tensor"),
            P(("groups", "page"), "tensor"),
        ),
        check_vma=False,
    )
```

time: 165 us -> 55.5 us (0.34)
  matrix products: 82.4 us -> 0 us
  Pallas kernels: 0 us -> 51.6 us
  waiting for transfers between devices: 40.4 us -> 0 us
  between operations: 14.2 us -> 0.65 us
  starting transfers between devices: 13.1 us -> 0 us
  local copies, waits for them, and re-layouts: 11.6 us -> 2.94 us
  other arithmetic: 2.64 us -> 0 us
    dot_general x13 -> x0, matrix products: 71.3 us -> none  [the longest x1 18.9 us: on_device(): jnp.einsum('htk,thd->khd', score_grad, query_heads, preferred_element_typ...]
    pallas_call x0 -> x3, Pallas kernels: none -> 51.6 us  [the longest x1 17.6 us: on_device(): pl.pallas_call(functools.partial(attend_kernel, pages), grid=(features //...]
    ppermute x4 -> x0, waiting for transfers between devices: 23.1 us -> none  [the longest x2 20.1 us: from_behind(): return lax.ppermute(x, axis, pairs)]
    all_gather x1 -> x0, waiting for transfers between devices: 17.2 us -> none  [on_device(): wide_memory = lax.all_gather(memory_rim, 'tensor', axis=1, tiled=True)]
    ppermute x4 -> x0, starting transfers between devices: 13 us -> none  [the longest x2 6.04 us: from_behind(): return lax.ppermute(x, axis, pairs)]
    sub x1 -> x0, matrix products: 11 us -> none  [on_device(): exponent = jnp.exp(scores - row_max)]
    reshape x3 -> x0, local copies, waits for them, and re-layouts: 6.42 us -> none  [the longest x1 2.64 us: on_device(): key_heads = key_slab.reshape(3 * memory_rows, head_count, HD)]
    slice x2 -> x0, local copies, waits for them, and re-layouts: 1.78 us -> none  [the longest x1 1.61 us: on_device(): key_piece[2 * memory_rows:]]
  transfers between devices with their start and end apart: 6 -> 0, of which waited for: 5 -> 0; matrix products, arithmetic and copies ran while one was open for 21% -> 0% of each run, Pallas kernels for 0% -> 0%
where the time goes in v1:
time: 55.5 us; the launch traced here: 55.1 us
  Pallas kernels  51.6 us (93%)
  local copies, waits for them, and re-layouts  2.94 us (5%)
  between operations  0.65 us (1%)
    pallas_call x1, Pallas kernels, on_device(): pl.pallas_call(functools.partial(attend_kernel, pages), grid=(features //...  17.6 us
    pallas_call x1, Pallas kernels, on_device(): pl.pallas_call(functools.partial(reduce_kernel, pages, tensors), out_shap...  17.5 us
    pallas_call x1, Pallas kernels, on_device(): pl.pallas_call(functools.partial(project_kernel, pages, tensors), out_sha...  16.4 us
    unnamed x2, local copies, waits for them, and re-layouts  2.94 us

profile of v1, /device:TPU:0, one launch (start us, length us, event | category | flops | bytes accessed | tf_op | source)
XLA Modules:
  0.0 55.1 jit_solution(2662213693511365932)
XLA Ops:
  0.6 1.4 %copy.9.mask_ref = s32[1,3,4,2]{3,2,1,0:T(4,128)} copy(s32[1,3,4,2]{2,3,1,0:T(2,128)} %param.11) | data formatting | bytes 192 | tf_op args[5]
  2.0 16.4 %gather_project.1 = (bf16[768,1024]{1,0:T(8,128)(2,1)}, bf16[768,1024]{1,0:T(8,128)(2,1)}) custom-call(bf16[256,256]{1,0:T(8,128)(2,1)} %mem_ref.1, bf16[1024,1024]{1,0:T(8,128)(2,1)} %wk_hbm.3, bf16[1024,1024]{1,0:T(8,128)(2,1)} %wv_hbm.3), custom_call_target="tpu_custom_call" | custom-call | tf_op jit(solution)/shard_map/gather_project/pallas_call | solution.py:351
  18.4 17.6 %attend.1 = (bf16[512,1024]{1,0:T(8,128)(2,1)}, bf16[512,1024]{1,0:T(8,128)(2,1)}, bf16[768,1024]{1,0:T(8,128)(2,1)}, bf16[768,1024]{1,0:T(8,128)(2,1)}) custom-call(s32[1,3,4,2]{3,2,1,0:T(4,128)} %copy.9.mask_ref, bf16[512,1024]{1,0:T(8,128)(2,1)} %q_ref.1, bf16[512,1024]{1,0:T(8,128)(2,1)} %g_ref.1, bf16[768,1024]{1,0:T(8,128)(2,1)} %get-tuple-element.9.k_ref, ...), custom_call_target="tpu_custom_call" | custom-call | tf_op jit(solution)/shard_map/attend/pallas_call | solution.py:376
  36.0 17.5 %back_project_reduce.1 = bf16[256,256]{1,0:T(8,128)(2,1)} custom-call(bf16[768,1024]{1,0:T(8,128)(2,1)} %get-tuple-element.13.kp_hbm, bf16[768,1024]{1,0:T(8,128)(2,1)} %get-tuple-element.14.vp_hbm, bf16[1024,1024]{1,0:T(8,128)(2,1)} %wk_hbm.3, bf16[1024,1024]{1,0:T(8,128)(2,1)} %wv_hbm.3), custom_call_target="tpu_custom_call" | custom-call | tf_op jit(solution)/shard_map/back_project_reduce/pallas_call | solution.py:398
  53.6 1.6 %copy.11 = bf16[256,256]{1,0:T(8,128)(2,1)} copy(bf16[256,256]{1,0:T(8,128)(2,1)} %back_project_reduce.1) | data formatting | bytes 262144

commit v2 on v1

--- a/solution.py
+++ b/solution.py
@@ -10,7 +10,8 @@
 
 HD = 128
 MESH = pl.DeviceIdType.MESH
-VMEM_LIMIT = 56 * 1024 * 1024
+VMEM_LIMIT = 24 * 1024 * 1024
+GATHER_LIMIT = 24 * 1024 * 1024
 F32 = jnp.float32
 BF16 = jnp.bfloat16
 
@@ -56,8 +57,8 @@
 
 
 def project_kernel(
-    pages, tensors, mem_ref, wk_hbm, wv_hbm, k_hbm, v_hbm,
-    gathered, wk, wv, keys, values, load_sem, store_sem, send_sem, recv_sem,
+    pages, tensors, mem_ref, wk_hbm, wv_hbm, keys, values,
+    gathered, wk, wv, load_sem, send_sem, recv_sem,
 ):
     page, tensor, core, sibling = place()
     chips = tensors // 2
@@ -115,26 +116,17 @@
         spread(gathered.at[1, owner], owner)
         to_sibling(gathered.at[1, owner], 1, owner).start()
 
-    stores = {}
-
     def project(slot):
+        span = slice(slot * rows, (slot + 1) * rows)
+
         def step(i, _):
             columns = pl.ds(pl.multiple_of(i * tile, tile), tile)
             whole = jnp.concatenate([gathered[slot, owner] for owner in range(tensors)], axis=1)
-            keys[slot, :, columns] = jnp.dot(whole, wk[:, columns], preferred_element_type=F32).astype(BF16)
-            values[slot, :, columns] = jnp.dot(whole, wv[:, columns], preferred_element_type=F32).astype(BF16)
+            keys[span, columns] = jnp.dot(whole, wk[:, columns], preferred_element_type=F32).astype(BF16)
+            values[span, columns] = jnp.dot(whole, wv[:, columns], preferred_element_type=F32).astype(BF16)
             return 0
 
         lax.fori_loop(0, features // tile, step, 0)
-
-    def write(slot):
-        span = pl.ds(slot * rows, rows)
-        stores[slot] = [
-            pltpu.make_async_copy(keys.at[slot], k_hbm.at[span], store_sem.at[slot, 0]),
-            pltpu.make_async_copy(values.at[slot], v_hbm.at[span], store_sem.at[slot, 1]),
-        ]
-        for store in stores[slot]:
-            store.start()
 
     def other(owner):
         return owner + 1 - 2 * lax.rem(owner, 2)
@@ -155,7 +147,6 @@
     for load in loads:
         load.wait()
     project(1)
-    write(1)
     for k in range(chips):
         pass_on(k)
     for slot, there in ((0, has_prev), (2, has_next)):
@@ -167,10 +158,9 @@
 
         @pl.when(jnp.logical_not(there))
         def _():
-            keys[slot] = jnp.zeros(keys.shape[1:], BF16)
-            values[slot] = jnp.zeros(values.shape[1:], BF16)
-
-        write(slot)
+            span = slice(slot * rows, (slot + 1) * rows)
+            keys[span] = jnp.zeros((rows, features), BF16)
+            values[span] = jnp.zeros((rows, features), BF16)
 
     for d in range(1, chips):
         to_chip(mem_ref, d).wait_send()
@@ -186,36 +176,47 @@
         def _():
             to_prev(mem_ref, owner).wait_send()
             to_sibling(mem_ref, 0, owner).wait_send()
-    for slot in (1, 0, 2):
-        for store in stores[slot]:
-            store.wait()
 
 
 def attend_kernel(pages, mask_ref, q_ref, g_ref, k_ref, v_ref, att_ref, qg_ref, kp_ref, vp_ref):
     page = lax.axis_index("page")
-    slots, query_blocks, memory_blocks = mask_ref.shape[1:]
+    slots, memory_blocks, query_blocks = mask_ref.shape[1:]
     block = q_ref.shape[0] // query_blocks
     scale = 1.0 / math.sqrt(HD)
     rate = scale * math.log2(math.e)
     nt = (((1,), (1,)), ((), ()))
     tn = (((0,), (0,)), ((), ()))
-    for head in range(q_ref.shape[1] // HD):
-        cols = slice(head * HD, (head + 1) * HD)
-        q, g, k, v = q_ref[:, cols], g_ref[:, cols], k_ref[:, cols], v_ref[:, cols]
-        scores = lax.dot_general(k, q, nt, preferred_element_type=F32)
-        weight_grad = lax.dot_general(v, g, nt, preferred_element_type=F32)
+    heads = q_ref.shape[1] // HD
+    bias = {}
+    for slot in range(slots):
+        source = page + (slot - 1)
+        live = jnp.logical_and(source >= 0, source < pages)
+        for tb in range(query_blocks):
+            for mb in range(memory_blocks):
+                seen = jnp.logical_and(mask_ref[0, slot, mb, tb] > 0, live)
+                bias[tb, slot * memory_blocks + mb] = jnp.where(seen, 0.0, -1e30).astype(F32)
+
+    def columns(head):
+        return slice(head * HD, (head + 1) * HD)
+
+    def products(head):
+        cols = columns(head)
+        return (
+            lax.dot_general(k_ref[:, cols], q_ref[:, cols], nt, preferred_element_type=F32),
+            lax.dot_general(v_ref[:, cols], g_ref[:, cols], nt, preferred_element_type=F32),
+        )
+
+    def softmax(scores, weight_grad):
         rounded, score_grads = [], []
         for tb in range(query_blocks):
             span = slice(tb * block, (tb + 1) * block)
-            parts = []
-            for slot in range(slots):
-                source = page + (slot - 1)
-                live = jnp.logical_and(source >= 0, source < pages)
-                for mb in range(memory_blocks):
-                    seen = jnp.logical_and(mask_ref[0, slot, tb, mb] > 0, live)
-                    low = (slot * memory_blocks + mb) * block
-                    parts.append(scores[low : low + block, span] + jnp.where(seen, 0.0, -1e30).astype(F32))
-            biased = jnp.concatenate(parts, axis=0)
+            biased = jnp.concatenate(
+                [
+                    scores[i * block : (i + 1) * block, span] + bias[tb, i]
+                    for i in range(slots * memory_blocks)
+                ],
+                axis=0,
+            )
             top = jnp.max(biased, axis=0, keepdims=True)
             exponent = jnp.exp2((biased - top) * rate)
             weights = exponent * (1.0 / jnp.sum(exponent, axis=0, keepdims=True))
@@ -223,20 +224,34 @@
             grad = weight_grad[:, span]
             inner = jnp.sum(weights * grad, axis=0, keepdims=True)
             score_grads.append((weights * (grad - inner)).astype(BF16))
-        rounded = jnp.concatenate(rounded, axis=1)
-        score_grad = jnp.concatenate(score_grads, axis=1)
-        att = lax.dot_general(v, rounded, tn, preferred_element_type=F32)
+        return jnp.concatenate(rounded, axis=1), jnp.concatenate(score_grads, axis=1)
+
+    def outputs(head, rounded, score_grad):
+        cols = columns(head)
+        att = lax.dot_general(v_ref[:, cols], rounded, tn, preferred_element_type=F32)
         att_ref[:, cols] = att.T.astype(BF16)
-        vp_ref[:, cols] = jnp.dot(rounded, g, preferred_element_type=F32).astype(BF16)
-        qg = lax.dot_general(k, score_grad, tn, preferred_element_type=F32) * scale
+        qg = lax.dot_general(k_ref[:, cols], score_grad, tn, preferred_element_type=F32) * scale
         qg_ref[:, cols] = qg.T.astype(BF16)
-        kp_ref[:, cols] = (jnp.dot(score_grad, q, preferred_element_type=F32) * scale).astype(BF16)
+        vp_ref[:, cols] = jnp.dot(rounded, g_ref[:, cols], preferred_element_type=F32).astype(BF16)
+        kp = jnp.dot(score_grad, q_ref[:, cols], preferred_element_type=F32) * scale
+        kp_ref[:, cols] = kp.astype(BF16)
+
+    ahead, ready = products(0), None
+    for head in range(heads):
+        now = ahead
+        if head + 1 < heads:
+            ahead = products(head + 1)
+        done = softmax(*now)
+        if ready is not None:
+            outputs(head - 1, *ready)
+        ready = done
+    outputs(heads - 1, *ready)
 
 
 def reduce_kernel(
-    pages, tensors, kp_hbm, vp_hbm, wk_hbm, wv_hbm, out_ref,
-    kp, vp, wk, wv, own, stage, from_core, page_stage, from_page, chip_stage, from_chip,
-    load_sem, core_send, core_recv, page_send, page_recv, chip_send, chip_recv,
+    pages, tensors, kp, vp, wk, wv, out_ref,
+    own, stage, from_core, page_stage, from_page, chip_stage, from_chip,
+    core_send, core_recv, page_send, page_recv, chip_send, chip_recv,
 ):
     page, tensor, core, sibling = place()
     chips = tensors // 2
@@ -244,15 +259,6 @@
     rows, width = out_ref.shape
     nt = (((1,), (1,)), ((), ()))
     wait_barrier = greet(pages, tensors)
-    loads = [
-        pltpu.make_async_copy(wk_hbm, wk, load_sem.at[0]),
-        pltpu.make_async_copy(kp_hbm, kp, load_sem.at[1]),
-        pltpu.make_async_copy(wv_hbm, wv, load_sem.at[2]),
-        pltpu.make_async_copy(vp_hbm, vp, load_sem.at[3]),
-    ]
-    for load in loads:
-        load.start()
-
     def partial(slot, group):
         take = pl.ds(pl.multiple_of(group * width, width), width)
         span = slice(slot * rows, (slot + 1) * rows)
@@ -286,30 +292,29 @@
 
     order = [lax.rem(chip + 1 + k, chips) for k in range(chips)]
 
-    def partials(slot, before_send=None):
-        for there in order:
-            stage[slot, there] = partial(slot, 2 * there + 1 - core).astype(BF16)
-            if before_send is not None:
-                before_send()
-                before_send = None
+    def for_core(slot, there):
+        stage[slot, there] = partial(slot, 2 * there + 1 - core).astype(BF16)
+
+    sides = (page > 0, page < pages - 1)
+    for there in order:
+        for slot in (0, 2):
+            for_core(slot, there)
+            if there is order[0] and slot == 0:
+                wait_barrier()
             to_core(slot, there).start()
-        for there in order:
+        for slot in (0, 2):
             own[slot, there] = partial(slot, 2 * there + core)
-
-    for load in loads:
-        load.wait()
-    sides = (page > 0, page < pages - 1)
-    for side in (0, 1):
-        slot = 2 * side
-        partials(slot, wait_barrier if side == 0 else None)
-        for there in order:
             to_core(slot, there).wait_recv()
 
-            @pl.when(sides[side])
+            @pl.when(sides[slot // 2])
             def _():
-                page_stage[side, there] = (own[slot, there] + from_core[slot, there].astype(F32)).astype(BF16)
-                to_page(side, there).start()
-    partials(1)
+                page_stage[slot // 2, there] = (own[slot, there] + from_core[slot, there].astype(F32)).astype(BF16)
+                to_page(slot // 2, there).start()
+    for there in order:
+        for_core(1, there)
+        to_core(1, there).start()
+    for there in order:
+        own[1, there] = partial(1, 2 * there + core)
     for there in order:
         to_core(1, there).wait_recv()
         own[1, there] += from_core[1, there].astype(F32)
@@ -345,32 +350,29 @@
     rows, width = memory.shape
     depth = key_weight.shape[0]
     chips = tensors // 2
-    anywhere = pl.BlockSpec(memory_space=pl.ANY)
     in_vmem = pl.BlockSpec(memory_space=pltpu.VMEM)
+    in_hbm = pl.BlockSpec(memory_space=pltpu.HBM)
     dma = pltpu.SemaphoreType.DMA
     keys, values = pl.pallas_call(
         functools.partial(project_kernel, pages, tensors),
         out_shape=[jax.ShapeDtypeStruct((3 * rows, features), BF16)] * 2,
-        in_specs=[in_vmem, anywhere, anywhere],
-        out_specs=[anywhere, anywhere],
+        in_specs=[in_vmem, in_hbm, in_hbm],
+        out_specs=[in_vmem, in_vmem],
         scratch_shapes=[
             pltpu.VMEM((3, tensors, rows, width), BF16),
             pltpu.VMEM((depth, features), BF16),
             pltpu.VMEM((depth, features), BF16),
-            pltpu.VMEM((3, rows, features), BF16),
-            pltpu.VMEM((3, rows, features), BF16),
             dma((2,)),
-            dma((3, 2)),
             dma((6, tensors)),
             dma((3, tensors)),
         ],
         compiler_params=pltpu.CompilerParams(
-            collective_id=0, has_side_effects=True, vmem_limit_bytes=VMEM_LIMIT
+            collective_id=0, has_side_effects=True, vmem_limit_bytes=GATHER_LIMIT
         ),
         name="gather_project",
-    )(memory, key_weight, value_weight)
-
-    heads = 1
+    )(memory, *[pltpu.with_memory_space_constraint(w, pltpu.HBM) for w in (key_weight, value_weight)])
+
+    heads = 2
     step = heads * HD
     column = lambda i: (0, i)
     attended, query_grad, key_piece, value_piece = pl.pallas_call(
@@ -393,18 +395,14 @@
         ],
         compiler_params=pltpu.CompilerParams(vmem_limit_bytes=VMEM_LIMIT),
         name="attend",
-    )(mask_blocks, query, out_grad, keys, values)
+    )(jnp.swapaxes(mask_blocks, 2, 3), query, out_grad, keys, values)
 
     memory_grad = pl.pallas_call(
         functools.partial(reduce_kernel, pages, tensors),
         out_shape=jax.ShapeDtypeStruct((rows, width), BF16),
-        in_specs=[anywhere] * 4,
+        in_specs=[in_vmem] * 4,
         out_specs=in_vmem,
         scratch_shapes=[
-            pltpu.VMEM((3 * rows, features), BF16),
-            pltpu.VMEM((3 * rows, features), BF16),
-            pltpu.VMEM((depth, features), BF16),
-            pltpu.VMEM((depth, features), BF16),
             pltpu.VMEM((3, chips, rows, width), F32),
             pltpu.VMEM((3, chips, rows, width), BF16),
             pltpu.VMEM((3, chips, rows, width), BF16),
@@ -412,7 +410,6 @@
             pltpu.VMEM((2, chips, rows, width), BF16),
             pltpu.VMEM((chips, rows, width), BF16),
             pltpu.VMEM((chips, rows, width), BF16),
-            dma((4,)),
             dma((3, chips)),
             dma((3, chips)),
             dma((2, chips)),

time: 55.5 us -> 47.7 us (0.86)
  Pallas kernels: 51.6 us -> 45.3 us
  local copies, waits for them, and re-layouts: 2.94 us -> 1.58 us
    pallas_call x1, Pallas kernels: 17.6 us -> 15 us  [on_device(): pl.pallas_call(functools.partial(attend_kernel, pages), grid=(features //...]
    pallas_call x1, Pallas kernels: 16.4 us -> 14.5 us  [on_device(): pl.pallas_call(functools.partial(project_kernel, pages, tensors), out_sha...]
    pallas_call x1, Pallas kernels: 17.5 us -> 15.8 us  [on_device(): pl.pallas_call(functools.partial(reduce_kernel, pages, tensors), out_shap...]
    unnamed x2 -> x13, local copies, waits for them, and re-layouts: 2.94 us -> 1.58 us
where the time goes in v2:
time: 47.7 us; the launch traced here: 47.6 us
  Pallas kernels  45.3 us (95%)
  local copies, waits for them, and re-layouts  1.58 us (3%)
  between operations  0.7 us (1%)
    pallas_call x1, Pallas kernels, on_device(): pl.pallas_call(functools.partial(reduce_kernel, pages, tensors), out_shap...  15.8 us
    pallas_call x1, Pallas kernels, on_device(): pl.pallas_call(functools.partial(attend_kernel, pages), grid=(features //...  15 us
    pallas_call x1, Pallas kernels, on_device(): pl.pallas_call(functools.partial(project_kernel, pages, tensors), out_sha...  14.5 us
    unnamed x13, local copies, waits for them, and re-layouts  1.58 us

profile of v2, /device:TPU:0, one launch (start us, length us, event | category | flops | bytes accessed | tf_op | source)
XLA Modules:
  0.0 47.6 jit_solution(5221291486751524696)
XLA Ops:
  0.6 0.0 copy-start.4
  0.6 0.9 %copy-done.4 = bf16[256,256]{1,0:T(8,128)(2,1)S(1)} copy-done((bf16[256,256]{1,0:T(8,128)(2,1)S(1)}, bf16[256,256]{1,0:T(8,128)(2,1)}, u32[]{:S(2)}) %copy-start.4) | copy-done | bytes 131096
  1.5 0.0 copy-start.2
  1.5 0.0 copy-start.3
  1.5 0.0 copy-start.5
  1.5 14.5 %gather_project.1 = (bf16[768,1024]{1,0:T(8,128)(2,1)S(1)}, bf16[768,1024]{1,0:T(8,128)(2,1)S(1)}) custom-call(bf16[256,256]{1,0:T(8,128)(2,1)S(1)} %copy-done.4, bf16[1024,1024]{1,0:T(8,128)(2,1)} %wk.1, bf16[1024,1024]{1,0:T(8,128)(2,1)} %wv.1), custom_call_target="tpu_custom_call" | custom-call | tf_op jit(solution)/shard_map/gather_project/pallas_call | solution.py:356
  16.0 0.0 copy-done.2
  16.0 0.0 copy-done.3
  16.1 0.0 copy-done.5
  16.1 0.0 copy-start
  16.1 0.0 copy-start.1
  16.1 15.0 %attend.1 = (bf16[512,1024]{1,0:T(8,128)(2,1)}, bf16[512,1024]{1,0:T(8,128)(2,1)}, bf16[768,1024]{1,0:T(8,128)(2,1)S(1)}, bf16[768,1024]{1,0:T(8,128)(2,1)S(1)}) custom-call(s32[1,3,2,4]{3,2,1,0:T(2,128)S(1)} %bitcast.1, bf16[512,1024]{1,0:T(8,128)(2,1)S(1)} %copy-done.2, bf16[512,1024]{1,0:T(8,128)(2,1)S(1)} %copy-done.3, ...), custom_call_target="tpu_custom_call" | custom-call | tf_op jit(solution)/shard_map/attend/pallas_call | solution.py:378
  31.1 0.0 copy-done
  31.1 0.0 copy-done.1
  31.1 15.8 %back_project_reduce.1 = bf16[256,256]{1,0:T(8,128)(2,1)S(1)} custom-call(bf16[768,1024]{1,0:T(8,128)(2,1)S(1)} %get-tuple-element.13.kp, bf16[768,1024]{1,0:T(8,128)(2,1)S(1)} %get-tuple-element.14.vp, bf16[1024,1024]{1,0:T(8,128)(2,1)S(1)} %copy-done, bf16[1024,1024]{1,0:T(8,128)(2,1)S(1)} %copy-done.1), custom_call_target="tpu_custom_call" | custom-call | tf_op jit(solution)/shard_map/back_project_reduce/pallas_call | solution.py:400
  46.9 0.7 %copy.10 = bf16[256,256]{1,0:T(8,128)(2,1)} copy(bf16[256,256]{1,0:T(8,128)(2,1)S(1)} %back_project_reduce.1) | data formatting | bytes 262144
Async XLA Ops:
  0.6 0.9 %copy-start.4 = (bf16[256,256]{1,0:T(8,128)(2,1)S(1)}, bf16[256,256]{1,0:T(8,128)(2,1)}, u32[]{:S(2)}) copy-start(bf16[256,256]{1,0:T(8,128)(2,1)} %mem_ref.1) | copy-start | bytes 393220
  1.5 14.5 %copy-start.2 = (bf16[512,1024]{1,0:T(8,128)(2,1)S(1)}, bf16[512,1024]{1,0:T(8,128)(2,1)}, u32[]{:S(2)}) copy-start(bf16[512,1024]{1,0:T(8,128)(2,1)} %q_ref.1) | copy-start | bytes 3145732
  1.5 14.5 %copy-start.3 = (bf16[512,1024]{1,0:T(8,128)(2,1)S(1)}, bf16[512,1024]{1,0:T(8,128)(2,1)}, u32[]{:S(2)}) copy-start(bf16[512,1024]{1,0:T(8,128)(2,1)} %g_ref.1) | copy-start | bytes 3145732
  1.5 14.5 %copy-start.5 = (s32[1,3,4,2]{2,3,1,0:T(2,128)S(1)}, s32[1,3,4,2]{2,3,1,0:T(2,128)}, u32[]{:S(2)}) copy-start(s32[1,3,4,2]{2,3,1,0:T(2,128)} %param.11) | copy-start | bytes 292
  16.1 15.0 %copy-start = (bf16[1024,1024]{1,0:T(8,128)(2,1)S(1)}, bf16[1024,1024]{1,0:T(8,128)(2,1)}, u32[]{:S(2)}) copy-start(bf16[1024,1024]{1,0:T(8,128)(2,1)} %wk.1) | copy-start | bytes 6291460
  16.1 15.0 %copy-start.1 = (bf16[1024,1024]{1,0:T(8,128)(2,1)S(1)}, bf16[1024,1024]{1,0:T(8,128)(2,1)}, u32[]{:S(2)}) copy-start(bf16[1024,1024]{1,0:T(8,128)(2,1)} %wv.1) | copy-start | bytes 6291460

commit v3 on v2

--- a/solution.py
+++ b/solution.py
@@ -67,13 +67,13 @@
     tile = min(256, features)
 
     loads = [
+        pltpu.make_async_copy(mem_ref, gathered.at[1, tensor], load_sem.at[2]),
         pltpu.make_async_copy(wk_hbm, wk, load_sem.at[0]),
         pltpu.make_async_copy(wv_hbm, wv, load_sem.at[1]),
     ]
     wait_barrier = greet(pages, tensors)
     for load in loads:
         load.start()
-    gathered[1, tensor] = mem_ref[...]
     has_prev = page > 0
     has_next = page < pages - 1
 
@@ -259,12 +259,16 @@
     rows, width = out_ref.shape
     nt = (((1,), (1,)), ((), ()))
     wait_barrier = greet(pages, tensors)
-    def partial(slot, group):
+    def partial(slots, group):
         take = pl.ds(pl.multiple_of(group * width, width), width)
-        span = slice(slot * rows, (slot + 1) * rows)
-        return lax.dot_general(kp[span], wk[take], nt, preferred_element_type=F32) + lax.dot_general(
-            vp[span], wv[take], nt, preferred_element_type=F32
+
+        def rows_of(piece):
+            return jnp.concatenate([piece[slot * rows : (slot + 1) * rows] for slot in slots], axis=0)
+
+        product = lax.dot_general(rows_of(kp), wk[take], nt, preferred_element_type=F32) + lax.dot_general(
+            rows_of(vp), wv[take], nt, preferred_element_type=F32
         )
+        return [product[i * rows : (i + 1) * rows] for i in range(len(slots))]
 
     def to_core(slot, there):
         return remote(
@@ -292,18 +296,22 @@
 
     order = [lax.rem(chip + 1 + k, chips) for k in range(chips)]
 
-    def for_core(slot, there):
-        stage[slot, there] = partial(slot, 2 * there + 1 - core).astype(BF16)
-
     sides = (page > 0, page < pages - 1)
-    for there in order:
+
+    def for_core(slots, there):
+        for slot, product in zip(slots, partial(slots, 2 * there + 1 - core)):
+            stage[slot, there] = product.astype(BF16)
+
+    for there in order:
+        for_core((0, 2), there)
+        if there is order[0]:
+            wait_barrier()
         for slot in (0, 2):
-            for_core(slot, there)
-            if there is order[0] and slot == 0:
-                wait_barrier()
             to_core(slot, there).start()
+        mine = partial((0, 2), 2 * there + core)
+        for slot, product in zip((0, 2), mine):
+            own[slot, there] = product
         for slot in (0, 2):
-            own[slot, there] = partial(slot, 2 * there + core)
             to_core(slot, there).wait_recv()
 
             @pl.when(sides[slot // 2])
@@ -311,10 +319,10 @@
                 page_stage[slot // 2, there] = (own[slot, there] + from_core[slot, there].astype(F32)).astype(BF16)
                 to_page(slot // 2, there).start()
     for there in order:
-        for_core(1, there)
+        for_core((1,), there)
         to_core(1, there).start()
     for there in order:
-        own[1, there] = partial(1, 2 * there + core)
+        own[1, there] = partial((1,), 2 * there + core)[0]
     for there in order:
         to_core(1, there).wait_recv()
         own[1, there] += from_core[1, there].astype(F32)
@@ -356,13 +364,13 @@
     keys, values = pl.pallas_call(
         functools.partial(project_kernel, pages, tensors),
         out_shape=[jax.ShapeDtypeStruct((3 * rows, features), BF16)] * 2,
-        in_specs=[in_vmem, in_hbm, in_hbm],
+        in_specs=[in_hbm] * 3,
         out_specs=[in_vmem, in_vmem],
         scratch_shapes=[
             pltpu.VMEM((3, tensors, rows, width), BF16),
             pltpu.VMEM((depth, features), BF16),
             pltpu.VMEM((depth, features), BF16),
-            dma((2,)),
+            dma((3,)),
             dma((6, tensors)),
             dma((3, tensors)),
         ],
@@ -370,7 +378,7 @@
             collective_id=0, has_side_effects=True, vmem_limit_bytes=GATHER_LIMIT
         ),
         name="gather_project",
-    )(memory, *[pltpu.with_memory_space_constraint(w, pltpu.HBM) for w in (key_weight, value_weight)])
+    )(*[pltpu.with_memory_space_constraint(a, pltpu.HBM) for a in (memory, key_weight, value_weight)])
 
     heads = 2
     step = heads * HD

time: 47.7 us -> 45.9 us (0.962)
  Pallas kernels: 45.3 us -> 44.3 us
  local copies, waits for them, and re-layouts: 1.58 us -> 0.68 us
    pallas_call x1, Pallas kernels: 15.8 us -> 14.5 us  [on_device(): pl.pallas_call(functools.partial(reduce_kernel, pages, tensors), out_shap...]
    unnamed x13 -> x11, local copies, waits for them, and re-layouts: 1.58 us -> 0.68 us
where the time goes in v3:
time: 45.9 us; the launch traced here: 45.7 us
  Pallas kernels  44.3 us (97%)
  between operations  0.71 us (2%)
  local copies, waits for them, and re-layouts  0.68 us (1%)
    pallas_call x1, Pallas kernels, on_device(): pl.pallas_call(functools.partial(attend_kernel, pages), grid=(features //...  15 us
    pallas_call x1, Pallas kernels, on_device(): pl.pallas_call(functools.partial(project_kernel, pages, tensors), out_sha...  14.8 us
    pallas_call x1, Pallas kernels, on_device(): pl.pallas_call(functools.partial(reduce_kernel, pages, tensors), out_shap...  14.5 us

profile of v3, /device:TPU:0, one launch (start us, length us, event | category | flops | bytes accessed | tf_op | source)
XLA Modules:
  0.0 45.7 jit_solution(3734066458446355761)
XLA Ops:
  0.6 0.0 copy-start.2
  0.6 0.0 copy-start.3
  0.7 0.0 copy-start.4
  0.7 14.8 %gather_project.1 = (bf16[768,1024]{1,0:T(8,128)(2,1)S(1)}, bf16[768,1024]{1,0:T(8,128)(2,1)S(1)}) custom-call(bf16[256,256]{1,0:T(8,128)(2,1)} %mem_ref.1, bf16[1024,1024]{1,0:T(8,128)(2,1)} %wk.1, bf16[1024,1024]{1,0:T(8,128)(2,1)} %wv.1), custom_call_target="tpu_custom_call" | custom-call | tf_op jit(solution)/shard_map/gather_project/pallas_call | solution.py:364
  15.4 0.0 copy-done.2
  15.5 0.0 copy-done.3
  15.5 0.0 copy-done.4
  15.5 0.0 copy-start
  15.5 0.0 copy-start.1
  15.5 15.0 %attend.1 = (bf16[512,1024]{1,0:T(8,128)(2,1)}, bf16[512,1024]{1,0:T(8,128)(2,1)}, bf16[768,1024]{1,0:T(8,128)(2,1)S(1)}, bf16[768,1024]{1,0:T(8,128)(2,1)S(1)}) custom-call(s32[1,3,2,4]{3,2,1,0:T(2,128)S(1)} %bitcast.1, bf16[512,1024]{1,0:T(8,128)(2,1)S(1)} %copy-done.2, bf16[512,1024]{1,0:T(8,128)(2,1)S(1)} %copy-done.3, ...), custom_call_target="tpu_custom_call" | custom-call | tf_op jit(solution)/shard_map/attend/pallas_call | solution.py:386
  30.5 0.0 copy-done
  30.5 0.0 copy-done.1
  30.5 14.5 %back_project_reduce.1 = bf16[256,256]{1,0:T(8,128)(2,1)S(1)} custom-call(bf16[768,1024]{1,0:T(8,128)(2,1)S(1)} %get-tuple-element.13.kp, bf16[768,1024]{1,0:T(8,128)(2,1)S(1)} %get-tuple-element.14.vp, bf16[1024,1024]{1,0:T(8,128)(2,1)S(1)} %copy-done, bf16[1024,1024]{1,0:T(8,128)(2,1)S(1)} %copy-done.1), custom_call_target="tpu_custom_call" | custom-call | tf_op jit(solution)/shard_map/back_project_reduce/pallas_call | solution.py:408
  45.1 0.7 %copy.10 = bf16[256,256]{1,0:T(8,128)(2,1)} copy(bf16[256,256]{1,0:T(8,128)(2,1)S(1)} %back_project_reduce.1) | data formatting | bytes 262144
Async XLA Ops:
  0.6 14.8 %copy-start.2 = (bf16[512,1024]{1,0:T(8,128)(2,1)S(1)}, bf16[512,1024]{1,0:T(8,128)(2,1)}, u32[]{:S(2)}) copy-start(bf16[512,1024]{1,0:T(8,128)(2,1)} %q_ref.1) | copy-start | bytes 3145732
  0.6 14.8 %copy-start.3 = (bf16[512,1024]{1,0:T(8,128)(2,1)S(1)}, bf16[512,1024]{1,0:T(8,128)(2,1)}, u32[]{:S(2)}) copy-start(bf16[512,1024]{1,0:T(8,128)(2,1)} %g_ref.1) | copy-start | bytes 3145732
  0.7 14.8 %copy-start.4 = (s32[1,3,4,2]{2,3,1,0:T(2,128)S(1)}, s32[1,3,4,2]{2,3,1,0:T(2,128)}, u32[]{:S(2)}) copy-start(s32[1,3,4,2]{2,3,1,0:T(2,128)} %param.11) | copy-start | bytes 292
  15.5 15.0 %copy-start = (bf16[1024,1024]{1,0:T(8,128)(2,1)S(1)}, bf16[1024,1024]{1,0:T(8,128)(2,1)}, u32[]{:S(2)}) copy-start(bf16[1024,1024]{1,0:T(8,128)(2,1)} %wk.1) | copy-start | bytes 6291460
  15.5 15.0 %copy-start.1 = (bf16[1024,1024]{1,0:T(8,128)(2,1)S(1)}, bf16[1024,1024]{1,0:T(8,128)(2,1)}, u32[]{:S(2)}) copy-start(bf16[1024,1024]{1,0:T(8,128)(2,1)} %wv.1) | copy-start | bytes 6291460

commit v4 on v3

--- a/solution.py
+++ b/solution.py
@@ -9,6 +9,7 @@
 from jax.sharding import PartitionSpec as P
 
 HD = 128
+HALVES = 2
 MESH = pl.DeviceIdType.MESH
 VMEM_LIMIT = 24 * 1024 * 1024
 GATHER_LIMIT = 24 * 1024 * 1024
@@ -77,53 +78,68 @@
     has_prev = page > 0
     has_next = page < pages - 1
 
-    def to_sibling(src, slot, owner):
-        return remote(src, gathered.at[slot, owner], send_sem.at[slot, owner], recv_sem.at[slot, owner], {"tensor": sibling})
-
-    def to_chip(src, d):
+    half = rows // HALVES
+
+    def part(ref, h):
+        return ref.at[pl.ds(h * half, half)]
+
+    def shard(slot, owner, h):
+        return gathered.at[slot, owner, pl.ds(h * half, half)]
+
+    def to_sibling(src, slot, owner, h):
+        return remote(src, shard(slot, owner, h), send_sem.at[slot, owner, h], recv_sem.at[slot, owner, h], {"tensor": sibling})
+
+    def to_chip(d, h):
         there = lax.rem(tensor + 2 * d, tensors)
-        return remote(src, gathered.at[1, tensor], send_sem.at[3, there], recv_sem.at[1, tensor], {"tensor": there})
-
-    def to_next(src, owner):
-        return remote(src, gathered.at[0, owner], send_sem.at[4, owner], recv_sem.at[0, owner], {"page": page + 1})
-
-    def to_prev(src, owner):
-        return remote(src, gathered.at[2, owner], send_sem.at[5, owner], recv_sem.at[2, owner], {"page": page - 1})
-
-    def arrived(slot, owner):
-        remote(
-            gathered.at[slot, owner], gathered.at[slot, owner], send_sem.at[0, owner],
-            recv_sem.at[slot, owner], {"tensor": sibling},
-        ).wait_recv()
-
-    def spread(src, owner):
+        return remote(part(mem_ref, h), shard(1, tensor, h), send_sem.at[3, there, h], recv_sem.at[1, tensor, h], {"tensor": there})
+
+    def to_next(src, owner, h):
+        return remote(src, shard(0, owner, h), send_sem.at[4, owner, h], recv_sem.at[0, owner, h], {"page": page + 1})
+
+    def to_prev(src, owner, h):
+        return remote(src, shard(2, owner, h), send_sem.at[5, owner, h], recv_sem.at[2, owner, h], {"page": page - 1})
+
+    def arrived(slot, owner, h):
+        here = shard(slot, owner, h)
+        remote(here, here, send_sem.at[0, owner, h], recv_sem.at[slot, owner, h], {"tensor": sibling}).wait_recv()
+
+    def spread(src, owner, h):
         @pl.when(has_next)
         def _():
-            to_next(src, owner).start()
+            to_next(src, owner, h).start()
 
         @pl.when(has_prev)
         def _():
-            to_prev(src, owner).start()
+            to_prev(src, owner, h).start()
 
     wait_barrier()
-    for d in range(1, chips):
-        to_chip(mem_ref, d).start()
-    spread(mem_ref, tensor)
-    to_sibling(mem_ref, 1, tensor).start()
+    for h in range(HALVES):
+        for d in range(1, chips):
+            to_chip(d, h).start()
+        spread(part(mem_ref, h), tensor, h)
+    for h in range(HALVES):
+        to_sibling(part(mem_ref, h), 1, tensor, h).start()
     peers = [lax.rem(tensor + 2 * d, tensors) for d in range(chips)]
     for owner in peers[1:]:
-        arrived(1, owner)
-        spread(gathered.at[1, owner], owner)
-        to_sibling(gathered.at[1, owner], 1, owner).start()
-
-    def project(slot):
-        span = slice(slot * rows, (slot + 1) * rows)
-
+        for h in range(HALVES):
+            arrived(1, owner, h)
+            spread(shard(1, owner, h), owner, h)
+            to_sibling(shard(1, owner, h), 1, owner, h).start()
+
+    def project(slots):
         def step(i, _):
             columns = pl.ds(pl.multiple_of(i * tile, tile), tile)
-            whole = jnp.concatenate([gathered[slot, owner] for owner in range(tensors)], axis=1)
-            keys[span, columns] = jnp.dot(whole, wk[:, columns], preferred_element_type=F32).astype(BF16)
-            values[span, columns] = jnp.dot(whole, wv[:, columns], preferred_element_type=F32).astype(BF16)
+            whole = jnp.concatenate(
+                [
+                    jnp.concatenate([gathered[slot, owner] for owner in range(tensors)], axis=1)
+                    for slot in slots
+                ],
+                axis=0,
+            )
+            for weight, out in ((wk, keys), (wv, values)):
+                product = jnp.dot(whole, weight[:, columns], preferred_element_type=F32).astype(BF16)
+                for j, slot in enumerate(slots):
+                    out[slot * rows : (slot + 1) * rows, columns] = product[j * rows : (j + 1) * rows]
             return 0
 
         lax.fori_loop(0, features // tile, step, 0)
@@ -131,51 +147,50 @@
     def other(owner):
         return owner + 1 - 2 * lax.rem(owner, 2)
 
-    def pass_on(k):
-        @pl.when(has_prev)
-        def _():
-            arrived(0, peers[k])
-            to_sibling(gathered.at[0, peers[k]], 0, peers[k]).start()
-
-        @pl.when(has_next)
-        def _():
-            arrived(2, peers[k])
-            to_sibling(gathered.at[2, peers[k]], 2, peers[k]).start()
+    def pass_on(owner, h):
+        for slot, there in ((0, has_prev), (2, has_next)):
+            @pl.when(there)
+            def _():
+                arrived(slot, owner, h)
+                to_sibling(shard(slot, owner, h), slot, owner, h).start()
 
     for owner in peers:
-        arrived(1, other(owner))
+        for h in range(HALVES):
+            arrived(1, other(owner), h)
     for load in loads:
         load.wait()
-    project(1)
-    for k in range(chips):
-        pass_on(k)
+    project((1,))
+    for owner in peers:
+        for h in range(HALVES):
+            pass_on(owner, h)
     for slot, there in ((0, has_prev), (2, has_next)):
         @pl.when(there)
         def _():
             for owner in peers:
-                arrived(slot, other(owner))
-            project(slot)
+                for h in range(HALVES):
+                    arrived(slot, other(owner), h)
 
         @pl.when(jnp.logical_not(there))
         def _():
-            span = slice(slot * rows, (slot + 1) * rows)
-            keys[span] = jnp.zeros((rows, features), BF16)
-            values[span] = jnp.zeros((rows, features), BF16)
-
-    for d in range(1, chips):
-        to_chip(mem_ref, d).wait_send()
-    for owner in peers:
-        to_sibling(mem_ref, 1, owner).wait_send()
-
-        @pl.when(has_next)
-        def _():
-            to_next(mem_ref, owner).wait_send()
-            to_sibling(mem_ref, 2, owner).wait_send()
-
-        @pl.when(has_prev)
-        def _():
-            to_prev(mem_ref, owner).wait_send()
-            to_sibling(mem_ref, 0, owner).wait_send()
+            gathered[slot] = jnp.zeros(gathered.shape[1:], BF16)
+
+    project((0, 2))
+    for h in range(HALVES):
+        for d in range(1, chips):
+            to_chip(d, h).wait_send()
+        for owner in peers:
+            src = part(mem_ref, h)
+            to_sibling(src, 1, owner, h).wait_send()
+
+            @pl.when(has_next)
+            def _():
+                to_next(src, owner, h).wait_send()
+                to_sibling(src, 2, owner, h).wait_send()
+
+            @pl.when(has_prev)
+            def _():
+                to_prev(src, owner, h).wait_send()
+                to_sibling(src, 0, owner, h).wait_send()
 
 
 def attend_kernel(pages, mask_ref, q_ref, g_ref, k_ref, v_ref, att_ref, qg_ref, kp_ref, vp_ref):
@@ -371,8 +386,8 @@
             pltpu.VMEM((depth, features), BF16),
             pltpu.VMEM((depth, features), BF16),
             dma((3,)),
-            dma((6, tensors)),
-            dma((3, tensors)),
+            dma((6, tensors, HALVES)),
+            dma((3, tensors, HALVES)),
         ],
         compiler_params=pltpu.CompilerParams(
             collective_id=0, has_side_effects=True, vmem_limit_bytes=GATHER_LIMIT

time: 45.9 us -> 45.6 us (level)
    pallas_call x1, Pallas kernels: 14.5 us -> 13.3 us  [on_device(): pl.pallas_call(functools.partial(reduce_kernel, pages, tensors), out_shap...]
    pallas_call x1, Pallas kernels: 14.8 us -> 15.7 us  [on_device(): pl.pallas_call(functools.partial(project_kernel, pages, tensors), out_sha...]
where the time goes in v4:
time: 45.6 us; the launch traced here: 45.4 us
  Pallas kernels  44 us (96%)
  between operations  0.71 us (2%)
  local copies, waits for them, and re-layouts  0.68 us (1%)
    pallas_call x1, Pallas kernels, on_device(): pl.pallas_call(functools.partial(project_kernel, pages, tensors), out_sha...  15.7 us
    pallas_call x1, Pallas kernels, on_device(): pl.pallas_call(functools.partial(attend_kernel, pages), grid=(features //...  15 us
    pallas_call x1, Pallas kernels, on_device(): pl.pallas_call(functools.partial(reduce_kernel, pages, tensors), out_shap...  13.3 us

profile of v4, /device:TPU:0, one launch (start us, length us, event | category | flops | bytes accessed | tf_op | source)
XLA Modules:
  0.0 45.4 jit_solution(5958046168139602910)
XLA Ops:
  0.6 0.0 copy-start.2
  0.6 0.0 copy-start.3
  0.7 0.0 copy-start.4
  0.7 15.7 %gather_project.1 = (bf16[768,1024]{1,0:T(8,128)(2,1)S(1)}, bf16[768,1024]{1,0:T(8,128)(2,1)S(1)}) custom-call(bf16[256,256]{1,0:T(8,128)(2,1)} %mem_ref.1, bf16[1024,1024]{1,0:T(8,128)(2,1)} %wk.1, bf16[1024,1024]{1,0:T(8,128)(2,1)} %wv.1), custom_call_target="tpu_custom_call" | custom-call | tf_op jit(solution)/shard_map/gather_project/pallas_call | solution.py:379
  16.4 0.0 copy-done.2
  16.4 0.0 copy-done.3
  16.4 0.0 copy-done.4
  16.4 0.0 copy-start
  16.4 0.0 copy-start.1
  16.4 15.0 %attend.1 = (bf16[512,1024]{1,0:T(8,128)(2,1)}, bf16[512,1024]{1,0:T(8,128)(2,1)}, bf16[768,1024]{1,0:T(8,128)(2,1)S(1)}, bf16[768,1024]{1,0:T(8,128)(2,1)S(1)}) custom-call(s32[1,3,2,4]{3,2,1,0:T(2,128)S(1)} %bitcast.1, bf16[512,1024]{1,0:T(8,128)(2,1)S(1)} %copy-done.2, bf16[512,1024]{1,0:T(8,128)(2,1)S(1)} %copy-done.3, ...), custom_call_target="tpu_custom_call" | custom-call | tf_op jit(solution)/shard_map/attend/pallas_call | solution.py:401
  31.4 0.0 copy-done
  31.4 0.0 copy-done.1
  31.4 13.3 %back_project_reduce.1 = bf16[256,256]{1,0:T(8,128)(2,1)S(1)} custom-call(bf16[768,1024]{1,0:T(8,128)(2,1)S(1)} %get-tuple-element.13.kp, bf16[768,1024]{1,0:T(8,128)(2,1)S(1)} %get-tuple-element.14.vp, bf16[1024,1024]{1,0:T(8,128)(2,1)S(1)} %copy-done, bf16[1024,1024]{1,0:T(8,128)(2,1)S(1)} %copy-done.1), custom_call_target="tpu_custom_call" | custom-call | tf_op jit(solution)/shard_map/back_project_reduce/pallas_call | solution.py:423
  44.8 0.7 %copy.10 = bf16[256,256]{1,0:T(8,128)(2,1)} copy(bf16[256,256]{1,0:T(8,128)(2,1)S(1)} %back_project_reduce.1) | data formatting | bytes 262144
Async XLA Ops:
  0.6 15.7 %copy-start.2 = (bf16[512,1024]{1,0:T(8,128)(2,1)S(1)}, bf16[512,1024]{1,0:T(8,128)(2,1)}, u32[]{:S(2)}) copy-start(bf16[512,1024]{1,0:T(8,128)(2,1)} %q_ref.1) | copy-start | bytes 3145732
  0.6 15.7 %copy-start.3 = (bf16[512,1024]{1,0:T(8,128)(2,1)S(1)}, bf16[512,1024]{1,0:T(8,128)(2,1)}, u32[]{:S(2)}) copy-start(bf16[512,1024]{1,0:T(8,128)(2,1)} %g_ref.1) | copy-start | bytes 3145732
  0.7 15.7 %copy-start.4 = (s32[1,3,4,2]{2,3,1,0:T(2,128)S(1)}, s32[1,3,4,2]{2,3,1,0:T(2,128)}, u32[]{:S(2)}) copy-start(s32[1,3,4,2]{2,3,1,0:T(2,128)} %param.11) | copy-start | bytes 292
  16.4 15.0 %copy-start = (bf16[1024,1024]{1,0:T(8,128)(2,1)S(1)}, bf16[1024,1024]{1,0:T(8,128)(2,1)}, u32[]{:S(2)}) copy-start(bf16[1024,1024]{1,0:T(8,128)(2,1)} %wk.1) | copy-start | bytes 6291460
  16.4 15.0 %copy-start.1 = (bf16[1024,1024]{1,0:T(8,128)(2,1)S(1)}, bf16[1024,1024]{1,0:T(8,128)(2,1)}, u32[]{:S(2)}) copy-start(bf16[1024,1024]{1,0:T(8,128)(2,1)} %wv.1) | copy-start | bytes 6291460

commit v5 on v4

--- a/solution.py
+++ b/solution.py
@@ -9,7 +9,7 @@
 from jax.sharding import PartitionSpec as P
 
 HD = 128
-HALVES = 2
+HALVES = 1
 MESH = pl.DeviceIdType.MESH
 VMEM_LIMIT = 24 * 1024 * 1024
 GATHER_LIMIT = 24 * 1024 * 1024

time: 45.6 us -> 45.9 us (level)
  no operation moved by 1% of the time
where the time goes in v5:
time: 45.9 us; the launch traced here: 45.8 us
  Pallas kernels  44.4 us (97%)
  between operations  0.71 us (2%)
  local copies, waits for them, and re-layouts  0.68 us (1%)
    pallas_call x1, Pallas kernels, on_device(): pl.pallas_call(functools.partial(project_kernel, pages, tensors), out_sha...  15.8 us
    pallas_call x1, Pallas kernels, on_device(): pl.pallas_call(functools.partial(attend_kernel, pages), grid=(features //...  15 us
    pallas_call x1, Pallas kernels, on_device(): pl.pallas_call(functools.partial(reduce_kernel, pages, tensors), out_shap...  13.6 us

profile of v5, /device:TPU:0, one launch (start us, length us, event | category | flops | bytes accessed | tf_op | source)
XLA Modules:
  0.0 45.8 jit_solution(4515561001550520643)
XLA Ops:
  0.6 0.0 copy-start.2
  0.6 0.0 copy-start.3
  0.7 0.0 copy-start.4
  0.7 15.8 %gather_project.1 = (bf16[768,1024]{1,0:T(8,128)(2,1)S(1)}, bf16[768,1024]{1,0:T(8,128)(2,1)S(1)}) custom-call(bf16[256,256]{1,0:T(8,128)(2,1)} %mem_ref.1, bf16[1024,1024]{1,0:T(8,128)(2,1)} %wk.1, bf16[1024,1024]{1,0:T(8,128)(2,1)} %wv.1), custom_call_target="tpu_custom_call" | custom-call | tf_op jit(solution)/shard_map/gather_project/pallas_call | solution.py:379
  16.5 0.0 copy-done.2
  16.5 0.0 copy-done.3
  16.5 0.0 copy-done.4
  16.5 0.0 copy-start
  16.5 0.0 copy-start.1
  16.5 15.0 %attend.1 = (bf16[512,1024]{1,0:T(8,128)(2,1)}, bf16[512,1024]{1,0:T(8,128)(2,1)}, bf16[768,1024]{1,0:T(8,128)(2,1)S(1)}, bf16[768,1024]{1,0:T(8,128)(2,1)S(1)}) custom-call(s32[1,3,2,4]{3,2,1,0:T(2,128)S(1)} %bitcast.1, bf16[512,1024]{1,0:T(8,128)(2,1)S(1)} %copy-done.2, bf16[512,1024]{1,0:T(8,128)(2,1)S(1)} %copy-done.3, ...), custom_call_target="tpu_custom_call" | custom-call | tf_op jit(solution)/shard_map/attend/pallas_call | solution.py:401
  31.5 0.0 copy-done
  31.5 0.0 copy-done.1
  31.6 13.6 %back_project_reduce.1 = bf16[256,256]{1,0:T(8,128)(2,1)S(1)} custom-call(bf16[768,1024]{1,0:T(8,128)(2,1)S(1)} %get-tuple-element.13.kp, bf16[768,1024]{1,0:T(8,128)(2,1)S(1)} %get-tuple-element.14.vp, bf16[1024,1024]{1,0:T(8,128)(2,1)S(1)} %copy-done, bf16[1024,1024]{1,0:T(8,128)(2,1)S(1)} %copy-done.1), custom_call_target="tpu_custom_call" | custom-call | tf_op jit(solution)/shard_map/back_project_reduce/pallas_call | solution.py:423
  45.1 0.7 %copy.10 = bf16[256,256]{1,0:T(8,128)(2,1)} copy(bf16[256,256]{1,0:T(8,128)(2,1)S(1)} %back_project_reduce.1) | data formatting | bytes 262144
Async XLA Ops:
  0.6 15.8 %copy-start.2 = (bf16[512,1024]{1,0:T(8,128)(2,1)S(1)}, bf16[512,1024]{1,0:T(8,128)(2,1)}, u32[]{:S(2)}) copy-start(bf16[512,1024]{1,0:T(8,128)(2,1)} %q_ref.1) | copy-start | bytes 3145732
  0.6 15.8 %copy-start.3 = (bf16[512,1024]{1,0:T(8,128)(2,1)S(1)}, bf16[512,1024]{1,0:T(8,128)(2,1)}, u32[]{:S(2)}) copy-start(bf16[512,1024]{1,0:T(8,128)(2,1)} %g_ref.1) | copy-start | bytes 3145732
  0.7 15.8 %copy-start.4 = (s32[1,3,4,2]{2,3,1,0:T(2,128)S(1)}, s32[1,3,4,2]{2,3,1,0:T(2,128)}, u32[]{:S(2)}) copy-start(s32[1,3,4,2]{2,3,1,0:T(2,128)} %param.11) | copy-start | bytes 292
  16.5 15.0 %copy-start = (bf16[1024,1024]{1,0:T(8,128)(2,1)S(1)}, bf16[1024,1024]{1,0:T(8,128)(2,1)}, u32[]{:S(2)}) copy-start(bf16[1024,1024]{1,0:T(8,128)(2,1)} %wk.1) | copy-start | bytes 6291460
  16.5 15.0 %copy-start.1 = (bf16[1024,1024]{1,0:T(8,128)(2,1)S(1)}, bf16[1024,1024]{1,0:T(8,128)(2,1)}, u32[]{:S(2)}) copy-start(bf16[1024,1024]{1,0:T(8,128)(2,1)} %wv.1) | copy-start | bytes 6291460
